TPU v7x, 32 devices: a whole 2x2x4 slice. The times are simulated.
32 devices in a mesh: dp: 2 (over y), fsdp: 16 (over z, x, core).
Axes of the slice: x: 2, y: 2, z: 4, core: 2. Of those that a mesh axis runs over, the one named last changes fastest.
Arguments:
- patches: bfloat16 [2, 32, 529, 768], P(None, ('dp', 'fsdp')), may hold values from -6 to 6
- visible_index: int32 [2, 32, 400], P(None, ('dp', 'fsdp')), may hold values from 0 to 528, as said below
- visible_count: int32 [2, 32], P(None, ('dp', 'fsdp')), may hold values from 389 to 400, as said below
- qkv_weight: bfloat16 [768, 2304], P(('dp', 'fsdp')), may hold values from -0.21875 to 0.21875
- out_weight: bfloat16 [768, 768], P(('dp', 'fsdp')), may hold values from -3.5 to 3.5
- up_weight: bfloat16 [768, 3072], P(('dp', 'fsdp')), may hold values from -0.21875 to 0.21875
- down_weight: bfloat16 [3072, 768], P(('dp', 'fsdp')), may hold values from -0.109375 to 0.109375
- attention_gain: bfloat16 [768], P(('dp', 'fsdp')), may hold values from 0.5 to 1.5
- attention_shift: bfloat16 [768], P(('dp', 'fsdp')), may hold values from -3 to 3
- feedforward_gain: bfloat16 [768], P(('dp', 'fsdp')), may hold values from 0.5 to 1.5
- feedforward_shift: bfloat16 [768], P(('dp', 'fsdp')), may hold values from -3 to 3
- cotangent: bfloat16 [2, 32, 400, 768], P(None, ('dp', 'fsdp')), may hold values from -6 to 6
Outputs:
- layer_output: float32 [2, 32, 400, 768], P(None, ('dp', 'fsdp'))
- patch_gradient: float32 [2, 32, 529, 768], P(None, ('dp', 'fsdp'))
- qkv_gradient: float32 [768, 2304], P(('dp', 'fsdp'))
- out_gradient: float32 [768, 768], P(('dp', 'fsdp'))
- up_gradient: float32 [768, 3072], P(('dp', 'fsdp'))
- down_gradient: float32 [3072, 768], P(('dp', 'fsdp'))
- attention_gain_gradient: float32 [768], P(('dp', 'fsdp'))
- attention_shift_gradient: float32 [768], P(('dp', 'fsdp'))
- feedforward_gain_gradient: float32 [768], P(('dp', 'fsdp'))
- feedforward_shift_gradient: float32 [768], P(('dp', 'fsdp'))
Inputs may be any that keep to these rules, and one draw needn't show every extreme that they name: `visible_index`: in each strip the first visible_count entries are the numbers of the visible patches in increasing order, each once; the other entries are numbers of masked patches. Masked patches gather near the start of the strip. `visible_count`: in each micro-batch some strip has exactly 400 visible patches.
All inputs are finite; a program needn't handle non-finite values.
Results may differ from a plain program's by a relative error of at most 0.012.
Values may be sent and summed in bfloat16 or wider, within the bound.
A program may use at most 192 MiB of HBM per device.

v0:
```python
import jax
import jax.numpy as jnp
from jax import lax
from jax.sharding import PartitionSpec as P

HEADS = 12


masked_score = -1000000000.0
norm_epsilon = 1e-06


def norm_forward(features, scaling, offset):
    center = features - jnp.mean(features, axis=-1, keepdims=True)
    inverse = lax.rsqrt(jnp.mean(center * center, axis=-1, keepdims=True) + norm_epsilon)
    normed = center * inverse
    return (normed * scaling.astype(jnp.float32) + offset.astype(jnp.float32), normed, inverse)


def norm_backward(upstream, normed, inverse, scaling):
    through = upstream * scaling.astype(jnp.float32)
    inward = inverse * (
        through
        - jnp.mean(through, axis=-1, keepdims=True)
        - normed * jnp.mean(through * normed, axis=-1, keepdims=True)
    )
    return (inward, jnp.sum(upstream * normed, axis=0), jnp.sum(upstream, axis=0))


def layer_forward(weights, patches, indices, counts):
    qkv_full, out_full, up_full, down_full, first_gain, first_shift, second_gain, second_shift = (
        weights
    )
    strips, visible, patch_count = (indices.shape[0], indices.shape[1], patches.shape[1])
    width = out_full.shape[1]
    present = jnp.arange(visible)[None, :] < counts[:, None]
    onehot = (
        (indices[:, :, None] == jnp.arange(patch_count)[None, None, :]) & present[:, :, None]
    ).astype(jnp.bfloat16)
    inputs = jnp.einsum(
        "bvp,bpd->bvd", onehot, patches, preferred_element_type=jnp.float32
    ).reshape(strips * visible, width)
    first_norm, first_normed, first_inverse = norm_forward(inputs, first_gain, first_shift)
    first_low = first_norm.astype(jnp.bfloat16)
    projected = jnp.dot(first_low, qkv_full, preferred_element_type=jnp.float32).astype(
        jnp.bfloat16
    )
    heads_shape = (strips, visible, HEADS, width // HEADS)
    queries = projected[:, :width].reshape(heads_shape)
    keys_low = projected[:, width : 2 * width].reshape(heads_shape)
    values_low = projected[:, 2 * width :].reshape(heads_shape)
    score_scale = (width // HEADS) ** (-0.5)
    scores = (
        jnp.einsum("bqhe,bkhe->bhqk", queries, keys_low, preferred_element_type=jnp.float32)
        * score_scale
    )
    scores = jnp.where(present[:, None, None, :], scores, masked_score)
    largest = jnp.max(scores, axis=-1, keepdims=True)
    exponent = jnp.exp(scores - largest)
    attention = exponent / jnp.sum(exponent, axis=-1, keepdims=True)
    attention_low = attention.astype(jnp.bfloat16)
    mixed_heads = jnp.einsum(
        "bhqk,bkhe->bqhe", attention_low, values_low, preferred_element_type=jnp.float32
    )
    mixed_heads = mixed_heads.astype(jnp.bfloat16).reshape(strips * visible, width)
    middle = inputs + jnp.dot(mixed_heads, out_full, preferred_element_type=jnp.float32)
    second_norm, second_normed, second_inverse = norm_forward(middle, second_gain, second_shift)
    second_low = second_norm.astype(jnp.bfloat16)
    hidden_pre = jnp.dot(second_low, up_full, preferred_element_type=jnp.float32)
    hidden_low = jax.nn.gelu(hidden_pre, approximate=False).astype(jnp.bfloat16)
    branch = jnp.dot(hidden_low, down_full, preferred_element_type=jnp.float32)
    present_rows = present.reshape(strips * visible, 1)
    output = (middle + branch) * present_rows.astype(jnp.float32)
    return {
        "onehot": onehot,
        "present_rows": present_rows,
        "first_low": first_low,
        "first_normed": first_normed,
        "first_inverse": first_inverse,
        "queries": queries,
        "keys_low": keys_low,
        "values_low": values_low,
        "attention": attention,
        "attention_low": attention_low,
        "mixed_heads": mixed_heads,
        "second_low": second_low,
        "second_normed": second_normed,
        "second_inverse": second_inverse,
        "hidden_pre": hidden_pre,
        "hidden_low": hidden_low,
        "output": output.reshape(strips, visible, width),
        "heads_shape": heads_shape,
        "score_scale": score_scale,
    }


def layer_backward(weights, patches, indices, counts, cotangent):
    qkv_full, out_full, up_full, down_full, first_gain, first_shift, second_gain, second_shift = (
        weights
    )
    stored = layer_forward(weights, patches, indices, counts)
    strips, visible = (indices.shape[0], indices.shape[1])
    width = out_full.shape[1]
    rows_all = strips * visible
    upstream = cotangent.reshape(rows_all, width) * stored["present_rows"].astype(jnp.bfloat16)
    down_grad = jnp.einsum(
        "rf,rd->fd", stored["hidden_low"], upstream, preferred_element_type=jnp.float32
    )
    hidden_grad = jnp.einsum("rd,fd->rf", upstream, down_full, preferred_element_type=jnp.float32)
    gelu_pull = jax.vjp(
        lambda values_in: jax.nn.gelu(values_in, approximate=False), stored["hidden_pre"]
    )[1]
    pre_low = gelu_pull(hidden_grad)[0].astype(jnp.bfloat16)
    up_grad = jnp.einsum(
        "rd,rf->df", stored["second_low"], pre_low, preferred_element_type=jnp.float32
    )
    second_back = jnp.einsum("rf,df->rd", pre_low, up_full, preferred_element_type=jnp.float32)
    middle_norm, second_gain_grad, second_shift_grad = norm_backward(
        second_back, stored["second_normed"], stored["second_inverse"], second_gain
    )
    middle_grad = upstream.astype(jnp.float32) + middle_norm
    middle_low = middle_grad.astype(jnp.bfloat16)
    out_grad = jnp.einsum(
        "rk,rd->kd", stored["mixed_heads"], middle_low, preferred_element_type=jnp.float32
    )
    mixed_grad = jnp.einsum("rd,kd->rk", middle_low, out_full, preferred_element_type=jnp.float32)
    mixed_grad = mixed_grad.astype(jnp.bfloat16).reshape(stored["heads_shape"])
    prob_grad = jnp.einsum(
        "bqhe,bkhe->bhqk", mixed_grad, stored["values_low"], preferred_element_type=jnp.float32
    )
    value_grad = jnp.einsum(
        "bhqk,bqhe->bkhe", stored["attention_low"], mixed_grad, preferred_element_type=jnp.float32
    )
    attention = stored["attention"]
    score_low = (
        attention * (prob_grad - jnp.sum(attention * prob_grad, axis=-1, keepdims=True))
    ).astype(jnp.bfloat16)
    query_grad = (
        jnp.einsum(
            "bhqk,bkhe->bqhe", score_low, stored["keys_low"], preferred_element_type=jnp.float32
        )
        * stored["score_scale"]
    )
    key_grad = (
        jnp.einsum(
            "bhqk,bqhe->bkhe", score_low, stored["queries"], preferred_element_type=jnp.float32
        )
        * stored["score_scale"]
    )
    projected_grad = jnp.concatenate(
        [
            query_grad.reshape(rows_all, width),
            key_grad.reshape(rows_all, width),
            value_grad.reshape(rows_all, width),
        ],
        axis=1,
    ).astype(jnp.bfloat16)
    qkv_grad = jnp.einsum(
        "rd,rc->dc", stored["first_low"], projected_grad, preferred_element_type=jnp.float32
    )
    first_back = jnp.einsum(
        "rc,dc->rd", projected_grad, qkv_full, preferred_element_type=jnp.float32
    )
    input_norm, first_gain_grad, first_shift_grad = norm_backward(
        first_back, stored["first_normed"], stored["first_inverse"], first_gain
    )
    input_low = (middle_grad + input_norm).astype(jnp.bfloat16).reshape(strips, visible, width)
    patch_part = jnp.einsum(
        "bvp,bvd->bpd", stored["onehot"], input_low, preferred_element_type=jnp.float32
    )
    gradients = (
        qkv_grad,
        out_grad,
        up_grad,
        down_grad,
        first_gain_grad,
        first_shift_grad,
        second_gain_grad,
        second_shift_grad,
    )
    return (gradients, patch_part)


def per_device(
    patches,
    visible_index,
    visible_count,
    qkv_weight,
    out_weight,
    up_weight,
    down_weight,
    attention_gain,
    attention_shift,
    feedforward_gain,
    feedforward_shift,
    cotangent,
):
    outputs_list = []
    patch_list = []
    shares = None
    for micro_step in range(patches.shape[0]):
        forward_full = (
            lax.all_gather(qkv_weight, ("dp", "fsdp"), axis=0, tiled=True),
            lax.all_gather(out_weight, ("dp", "fsdp"), axis=0, tiled=True),
            lax.all_gather(up_weight, ("dp", "fsdp"), axis=0, tiled=True),
            lax.all_gather(down_weight, ("dp", "fsdp"), axis=0, tiled=True),
            lax.all_gather(attention_gain, ("dp", "fsdp"), axis=0, tiled=True),
            lax.all_gather(attention_shift, ("dp", "fsdp"), axis=0, tiled=True),
            lax.all_gather(feedforward_gain, ("dp", "fsdp"), axis=0, tiled=True),
            lax.all_gather(feedforward_shift, ("dp", "fsdp"), axis=0, tiled=True),
        )
        stored = layer_forward(
            forward_full, patches[micro_step], visible_index[micro_step], visible_count[micro_step]
        )
        outputs_list.append(stored["output"])
        backward_full = (
            lax.all_gather(qkv_weight, ("dp", "fsdp"), axis=0, tiled=True),
            lax.all_gather(out_weight, ("dp", "fsdp"), axis=0, tiled=True),
            lax.all_gather(up_weight, ("dp", "fsdp"), axis=0, tiled=True),
            lax.all_gather(down_weight, ("dp", "fsdp"), axis=0, tiled=True),
            lax.all_gather(attention_gain, ("dp", "fsdp"), axis=0, tiled=True),
            lax.all_gather(attention_shift, ("dp", "fsdp"), axis=0, tiled=True),
            lax.all_gather(feedforward_gain, ("dp", "fsdp"), axis=0, tiled=True),
            lax.all_gather(feedforward_shift, ("dp", "fsdp"), axis=0, tiled=True),
        )
        gradients, patch_part = layer_backward(
            backward_full,
            patches[micro_step],
            visible_index[micro_step],
            visible_count[micro_step],
            cotangent[micro_step],
        )
        patch_list.append(patch_part)
        pieces = (
            lax.psum_scatter(gradients[0], ("dp", "fsdp"), scatter_dimension=0, tiled=True),
            lax.psum_scatter(gradients[1], ("dp", "fsdp"), scatter_dimension=0, tiled=True),
            lax.psum_scatter(gradients[2], ("dp", "fsdp"), scatter_dimension=0, tiled=True),
            lax.psum_scatter(gradients[3], ("dp", "fsdp"), scatter_dimension=0, tiled=True),
            lax.psum_scatter(gradients[4], ("dp", "fsdp"), scatter_dimension=0, tiled=True),
            lax.psum_scatter(gradients[5], ("dp", "fsdp"), scatter_dimension=0, tiled=True),
            lax.psum_scatter(gradients[6], ("dp", "fsdp"), scatter_dimension=0, tiled=True),
            lax.psum_scatter(gradients[7], ("dp", "fsdp"), scatter_dimension=0, tiled=True),
        )
        shares = pieces if shares is None else jax.tree.map(jnp.add, shares, pieces)
    return (
        jnp.stack(outputs_list),
        jnp.stack(patch_list),
        shares[0],
        shares[1],
        shares[2],
        shares[3],
        shares[4],
        shares[5],
        shares[6],
        shares[7],
    )


def solution(mesh):
    in_specs = (
        P(None, ("dp", "fsdp"), None, None),
        P(None, ("dp", "fsdp"), None),
        P(None, ("dp", "fsdp")),
        P(("dp", "fsdp"), None),
        P(("dp", "fsdp"), None),
        P(("dp", "fsdp"), None),
        P(("dp", "fsdp"), None),
        P(("dp", "fsdp")),
        P(("dp", "fsdp")),
        P(("dp", "fsdp")),
        P(("dp", "fsdp")),
        P(None, ("dp", "fsdp"), None, None),
    )
    out_specs = (
        P(None, ("dp", "fsdp"), None, None),
        P(None, ("dp", "fsdp"), None, None),
        P(("dp", "fsdp"), None),
        P(("dp", "fsdp"), None),
        P(("dp", "fsdp"), None),
        P(("dp", "fsdp"), None),
        P(("dp", "fsdp")),
        P(("dp", "fsdp")),
        P(("dp", "fsdp")),
        P(("dp", "fsdp")),
    )
    return jax.shard_map(
        per_device, mesh=mesh, in_specs=in_specs, out_specs=out_specs, check_vma=False
    )
```

profile of v0, /device:TPU:0, one launch (start us, length us, event | category | flops | bytes accessed | tf_op | source)
XLA Modules:
  0.0 863.2 jit_solution(6128336011155029770)
XLA Ops:
  17.4 42.2 %all-reduce.9 = (bf16[768]{0:T(1024)(128)(2,1)S(1)}, bf16[768]{0:T(1024)(128)(2,1)S(1)}, bf16[768]{0:T(1024)(128)(2,1)S(1)}, bf16[768]{0:T(1024)(128)(2,1)S(1)}) all-reduce(bf16[768]{0:T(1024)(128)(2,1)S(1)} %dynamic-update-slice.1, bf16[768]{0:T(1024)(128)(2,1)S(1)} %dynamic-update-slice, ...), channel_id=1, replica_groups=mesh['dp'=2,'fsdp'=16] {'dp','fsdp'}, use_global_device_ids=true, to_apply=%add.1 | all-reduce | flops 3072 | bytes 12288
  67.7 6.1 all-gather.5.cloned.1.call-done
  96.4 9.0 %fusion.121 = (f32[12,400]{1,0:T(8,128)S(1)}, f32[12,400,400]{1,2,0:T(8,128)}) fusion(pred[400]{0:T(512)(128)(4,1)S(1)} %iota_compare_fusion.5, bf16[400,12,64]{0,2,1:T(8,128)(2,1)} %bitcast.154, bf16[400,12,64]{0,2,1:T(8,128)(2,1)S(1)} %bitcast.152), kind=kOutput, calls=%fused_computation.213 | convolution fusion | flops 253440400 | bytes 8928400 | tf_op jit(solution)/shard_map/sub | solution.py:59
  105.4 6.0 fusion.30
  111.4 18.3 %all-gather.7.cloned.1.call-done = bf16[768,768]{1,0:T(8,128)(2,1)} async-done(((bf16[24,768]{1,0:T(8,128)(2,1)}), bf16[768,768]{1,0:T(8,128)(2,1)}) %all-gather.7.cloned.1.call-update) | async-done | bytes 1179664 | tf_op jit(solution)/shard_map/all_gather | solution.py:204
  133.5 9.1 %fusion.118 = (f32[12,400]{1,0:T(8,128)S(1)}, f32[12,400,400]{1,2,0:T(8,128)}) fusion(pred[400]{0:T(512)(128)(4,1)S(1)} %iota_compare_fusion.4, bf16[400,12,64]{0,2,1:T(8,128)(2,1)} %bitcast.158, bf16[400,12,64]{0,2,1:T(8,128)(2,1)S(1)} %bitcast.156), kind=kOutput, calls=%fused_computation.210 | convolution fusion | flops 253440400 | bytes 8928400 | tf_op jit(solution)/shard_map/sub | solution.py:59
  148.7 46.4 %all-gather.9.cloned.1.call-done = bf16[768,3072]{1,0:T(8,128)(2,1)} async-done(((bf16[24,3072]{1,0:T(8,128)(2,1)}), bf16[768,3072]{1,0:T(8,128)(2,1)}) %all-gather.9.cloned.1.call-update) | async-done | bytes 4718608 | tf_op jit(solution)/shard_map/all_gather | solution.py:205
  195.1 15.7 %multiply_convert_fusion.2 = (bf16[400,3072]{1,0:T(8,128)(2,1)}, f32[400,3072]{1,0:T(8,128)}, f32[400,3072]{1,0:T(8,128)}) fusion(bf16[768,3072]{1,0:T(8,128)(2,1)} %all-gather.9.cloned.1.call-done, f32[400,768]{1,0:T(8,128)S(1)} %get-tuple-element.95, f32[400]{0:T(512)S(1)} %add_rsqrt_fusion, f32[400]{0:T(512)S(1)} %broadcast_multiply_fusion.8, ...), kind=kOutput, calls=%fused_computation.21 | convolution fusion | flops 1968844800 | bytes 18244736 | tf_op jit(solution)/shard_map/dot_general | solution.py:69
  210.7 49.5 %all-gather.11.cloned.1.call-done = bf16[3072,768]{1,0:T(8,128)(2,1)} async-done(((bf16[96,768]{1,0:T(8,128)(2,1)}), bf16[3072,768]{1,0:T(8,128)(2,1)}) %all-gather.11.cloned.1.call-update) | async-done | bytes 4718608 | tf_op jit(solution)/shard_map/all_gather | solution.py:206
  260.2 8.0 add_convert_fusion
  270.5 15.6 %multiply_convert_fusion.3 = (bf16[400,3072]{1,0:T(8,128)(2,1)}, f32[400,3072]{1,0:T(8,128)}, f32[400,3072]{1,0:T(8,128)}) fusion(bf16[768,3072]{1,0:T(8,128)(2,1)S(1)} %copy-done.62, f32[400,768]{1,0:T(8,128)S(1)} %copy-done.14, f32[768]{0:T(1024)S(1)} %convert_element_type.175, f32[768]{0:T(1024)S(1)} %convert_element_type.174, ...), kind=kOutput, calls=%fused_computation.35 | convolution fusion | flops 1968844800 | bytes 18244736 | tf_op jit(solution)/shard_map/dot_general | solution.py:69
  286.1 6.4 add_convert_fusion.1
  299.5 9.5 %multiply_reduce_fusion = (f32[12,400]{1,0:T(8,128)S(1)}, f32[12,400,400]{1,2,0:T(8,128)}) fusion(f32[12,400,400]{1,2,0:T(8,128)} %get-tuple-element.93, f32[12,400]{1,0:T(8,128)S(1)} %get-tuple-element.92, bf16[400,12,64]{0,2,1:T(8,128)(2,1)} %bitcast.174, bf16[400,12,64]{0,2,1:T(8,128)(2,1)} %bitcast.172), kind=kOutput, calls=%fused_computation.3 | convolution fusion | flops 251515200 | bytes 16627200 | tf_op jit(solution)/shard_map/bqhe,bkhe->bhqk/dot_general | solution.py:128
  309.0 11.7 %multiply_convert_fusion = bf16[12,400,400]{1,2,0:T(8,128)(2,1)} fusion(f32[12,400,400]{1,2,0:T(8,128)} %get-tuple-element.106, f32[12,400]{1,0:T(8,128)S(1)} %get-tuple-element.105, f32[12,400,400]{1,2,0:T(8,128)} %get-tuple-element.93, f32[12,400]{1,0:T(8,128)S(1)} %get-tuple-element.92), kind=kLoop, calls=%fused_computation.2 | loop fusion | flops 7680000 | bytes 19238400 | tf_op jit(solution)/shard_map/convert_element_type | solution.py:137
  333.0 6.6 fusion.33
  339.6 7.3 multiply_reduce_fusion.1
  349.4 11.7 %multiply_convert_fusion.1 = bf16[12,400,400]{1,2,0:T(8,128)(2,1)} fusion(f32[12,400,400]{1,2,0:T(8,128)} %get-tuple-element.108, f32[12,400]{1,0:T(8,128)S(1)} %get-tuple-element.107, f32[12,400,400]{1,2,0:T(8,128)} %get-tuple-element.100, f32[12,400]{1,0:T(8,128)S(1)} %copy-done.47), kind=kLoop, calls=%fused_computation.4 | loop fusion | flops 7680000 | bytes 19238400 | tf_op jit(solution)/shard_map/convert_element_type | solution.py:137
  369.8 5.6 fusion.39
  387.1 5.6 convolution_add_fusion.2
  397.6 5.6 convolution_add_fusion.1
  421.0 40.2 %all-reduce.8 = (f32[768]{0:T(1024)S(1)}, f32[768]{0:T(1024)S(1)}, f32[768]{0:T(1024)S(1)}, f32[768]{0:T(1024)S(1)}) all-reduce(f32[768]{0:T(1024)S(1)} %add.192, f32[768]{0:T(1024)S(1)} %add.193, f32[768]{0:T(1024)S(1)} %add.194, f32[768]{0:T(1024)S(1)} %add.195), channel_id=14, replica_groups=mesh['dp'=2,'fsdp'=16] {'dp','fsdp'}, use_global_device_ids=true, to_apply=%region_31.32.clone | all-reduce | flops 3072 | bytes 24576
  475.3 97.1 %reduce-scatter.5.cloned.1.call-done = f32[24,2304]{1,0:T(8,128)} async-done(((f32[768,2304]{1,0:T(8,128)}), f32[24,2304]{1,0:T(8,128)}) %reduce-scatter.5.cloned.1.call-update) | async-done | bytes 221200 | tf_op jit(solution)/shard_map/reduce_scatter | solution.py:235
  572.4 141.2 %reduce-scatter.9.cloned.1.call-done = f32[24,3072]{1,0:T(8,128)} async-done(((f32[768,3072]{1,0:T(8,128)}), f32[24,3072]{1,0:T(8,128)}) %reduce-scatter.9.cloned.1.call-update) | async-done | bytes 294928 | tf_op jit(solution)/shard_map/reduce_scatter | solution.py:237
  713.6 142.2 %reduce-scatter.11.cloned.1.call-done = f32[96,768]{1,0:T(8,128)} async-done(((f32[3072,768]{1,0:T(8,128)}), f32[96,768]{1,0:T(8,128)}) %reduce-scatter.11.cloned.1.call-update) | async-done | bytes 294928 | tf_op jit(solution)/shard_map/reduce_scatter | solution.py:238
  (248 shorter events, 130.8 us)
Async XLA Ops:
  7.2 66.6 %all-gather.5.cloned.1.call-start = ((), (), s32[]{:S(2)}) async-start(), calls=%async_computation.4 | async-start | bytes 3649536 | tf_op jit(solution)/shard_map/all_gather | solution.py:203
  7.9 121.7 %all-gather.7.cloned.1.call-start = ((), (), s32[]{:S(2)}) async-start(), calls=%async_computation.5 | async-start | bytes 1216512 | tf_op jit(solution)/shard_map/all_gather | solution.py:204
  8.7 186.4 %all-gather.9.cloned.1.call-start = ((), (), s32[]{:S(2)}) async-start(), calls=%async_computation.6 | async-start | bytes 4866048 | tf_op jit(solution)/shard_map/all_gather | solution.py:205
  9.4 250.8 %all-gather.11.cloned.1.call-start = ((), (), s32[]{:S(2)}) async-start(), calls=%async_computation.7 | async-start | bytes 4866048 | tf_op jit(solution)/shard_map/all_gather | solution.py:206
  10.0 465.3 %reduce-scatter.7.cloned.1.call-start = ((), (), s32[]{:S(2)}) async-start(), calls=%async_computation.9 | async-start | bytes 2433024 | tf_op jit(solution)/shard_map/reduce_scatter | solution.py:236
  12.0 84.4 %copy-start.58 = (pred[400]{0:T(512)(128)(4,1)}, pred[400]{0:T(512)(128)(4,1)S(1)}, u32[]{:S(2)}) copy-start(pred[400]{0:T(512)(128)(4,1)S(1)} %iota_compare_fusion.5) | copy-start | bytes 1204
  13.3 120.1 %copy-start.60 = (pred[400]{0:T(512)(128)(4,1)}, pred[400]{0:T(512)(128)(4,1)S(1)}, u32[]{:S(2)}) copy-start(pred[400]{0:T(512)(128)(4,1)S(1)} %iota_compare_fusion.4) | copy-start | bytes 1204
  59.6 18.1 %copy-start.42 = (f32[768]{0:T(1024)}, f32[768]{0:T(1024)S(1)}, u32[]{:S(2)}) copy-start(f32[768]{0:T(1024)S(1)} %convert_element_type.167) | copy-start | bytes 9220
  59.6 18.1 %copy-start.40 = (f32[768]{0:T(1024)}, f32[768]{0:T(1024)S(1)}, u32[]{:S(2)}) copy-start(f32[768]{0:T(1024)S(1)} %convert_element_type.166) | copy-start | bytes 9220
  66.2 63.5 %copy-start.10 = (f32[400,768]{1,0:T(8,128)}, f32[400,768]{1,0:T(8,128)S(1)}, u32[]{:S(2)}) copy-start(f32[400,768]{1,0:T(8,128)S(1)} %get-tuple-element.98) | copy-start | bytes 3686404
  66.2 11.5 %copy-start.50 = (f32[400]{0:T(512)}, f32[400]{0:T(512)S(1)}, u32[]{:S(2)}) copy-start(f32[400]{0:T(512)S(1)} %broadcast_multiply_fusion.11) | copy-start | bytes 4804
  66.5 11.2 %copy-start.52 = (f32[400]{0:T(512)}, f32[400]{0:T(512)S(1)}, u32[]{:S(2)}) copy-start(f32[400]{0:T(512)S(1)} %add_rsqrt_fusion.3) | copy-start | bytes 4804
  67.3 80.2 %copy-start.4 = (f32[400,768]{1,0:T(8,128)}, f32[400,768]{1,0:T(8,128)S(1)}, u32[]{:S(2)}) copy-start(f32[400,768]{1,0:T(8,128)S(1)} %get-tuple-element.91) | copy-start | bytes 3686404
  67.4 10.3 %copy-start.44 = (f32[400]{0:T(512)}, f32[400]{0:T(512)S(1)}, u32[]{:S(2)}) copy-start(f32[400]{0:T(512)S(1)} %broadcast_multiply_fusion.9) | copy-start | bytes 4804
  67.7 10.1 %copy-start.48 = (f32[400]{0:T(512)}, f32[400]{0:T(512)S(1)}, u32[]{:S(2)}) copy-start(f32[400]{0:T(512)S(1)} %add_rsqrt_fusion.1) | copy-start | bytes 4804
  91.6 13.8 %copy-start.19 = (bf16[400,768]{0,1:T(8,128)(2,1)}, bf16[400,768]{0,1:T(8,128)(2,1)S(1)}, u32[]{:S(2)}) copy-start(bf16[400,768]{0,1:T(8,128)(2,1)S(1)} %copy.69) | copy-start | bytes 1843204
  111.4 22.1 %copy-start.21 = (bf16[400,768]{0,1:T(8,128)(2,1)S(1)}, bf16[400,768]{0,1:T(8,128)(2,1)}, u32[]{:S(2)}) copy-start(bf16[400,768]{0,1:T(8,128)(2,1)} %copy.74) | copy-start | bytes 1843204
  133.5 9.1 %copy-start.37 = (bf16[400,768]{0,1:T(8,128)(2,1)S(1)}, bf16[400,768]{0,1:T(8,128)(2,1)}, u32[]{:S(2)}) copy-start(bf16[400,768]{0,1:T(8,128)(2,1)} %copy.72) | copy-start | bytes 1843204
  148.7 111.5 %copy-start.26 = (bf16[2,1,400,768]{3,2,1,0:T(8,128)(2,1)S(1)}, bf16[2,1,400,768]{3,2,1,0:T(8,128)(2,1)}, u32[]{:S(2)}) copy-start(bf16[2,1,400,768]{3,2,1,0:T(8,128)(2,1)} %param.23) | copy-start | bytes 3686404
  268.3 17.8 %slice-start = ((s8[4718592]{0:T(1024)(128)(4,1)}), s8[4194304]{0:T(1024)(128)(4,1)S(1)}, s32[]{:S(2)}) async-start(s8[4718592]{0:T(1024)(128)(4,1)} %bitcast.182), calls=%async_computation.12 | async-start | bytes 8388608
  270.5 15.6 %slice-start.1 = ((s8[4718592]{0:T(1024)(128)(4,1)}), s8[524288]{0:T(1024)(128)(4,1)S(1)}, s32[]{:S(2)}) async-start(s8[4718592]{0:T(1024)(128)(4,1)} %bitcast.182), calls=%async_computation.13 | async-start | bytes 1048576
  349.2 223.2 %reduce-scatter.5.cloned.1.call-start = ((), (), s32[]{:S(2)}) async-start(), calls=%async_computation.8 | async-start | bytes 7299072 | tf_op jit(solution)/shard_map/reduce_scatter | solution.py:235
  381.8 331.9 %reduce-scatter.9.cloned.1.call-start = ((), (), s32[]{:S(2)}) async-start(), calls=%async_computation.10 | async-start | bytes 9732096 | tf_op jit(solution)/shard_map/reduce_scatter | solution.py:237
  392.8 463.1 %reduce-scatter.11.cloned.1.call-start = ((), (), s32[]{:S(2)}) async-start(), calls=%async_computation.11 | async-start | bytes 9732096 | tf_op jit(solution)/shard_map/reduce_scatter | solution.py:238
  (55 other events, 215.4 us)
Sparse Core Ops, SparseCore 0:
  10.9 62.8 all-gather.4
  76.7 52.9 all-gather.6
  132.5 62.5 all-gather.8
  197.8 62.3 all-gather.10
  349.3 97.8 reduce-scatter.6
  454.2 118.1 reduce-scatter.4
  578.9 134.7 reduce-scatter.8
  721.1 134.7 reduce-scatter.10
where the time goes:
time: 867 us; the launch traced here: 863 us
  waiting for transfers between devices  503 us (58%)
  matrix products  188 us (22%)
  blocking collectives  82.4 us (10%)
  local copies, waits for them, and re-layouts  40.2 us (5%)
  other arithmetic  32.7 us (4%)
  between operations  15.7 us (2%)
    reduce_scatter x1, waiting for transfers between devices, per_device(): lax.psum_scatter(gradients[3], ('dp', 'fsdp'), scatter_dimension=0, tiled...  142 us
    reduce_scatter x1, waiting for transfers between devices, per_device(): lax.psum_scatter(gradients[2], ('dp', 'fsdp'), scatter_dimension=0, tiled...  141 us
    reduce_scatter x1, waiting for transfers between devices, per_device(): lax.psum_scatter(gradients[0], ('dp', 'fsdp'), scatter_dimension=0, tiled...  97.1 us
    unnamed x2, blocking collectives  82.4 us
    all_gather x1, waiting for transfers between devices, per_device(): lax.all_gather(down_weight, ('dp', 'fsdp'), axis=0, tiled=True)  49.5 us
    all_gather x1, waiting for transfers between devices, per_device(): lax.all_gather(up_weight, ('dp', 'fsdp'), axis=0, tiled=True)  46.4 us
    dot_general x2, matrix products, layer_forward(): jnp.dot(second_low, up_full, preferred_element_type=jnp.float32)  31.2 us
    convert_element_type x2, other arithmetic, layer_backward(): score_low = (attention * (prob_grad - jnp.sum(attention * prob_grad, axis...  23.4 us
  transfers between devices with their start and end apart: 8, of which 7 were waited for; matrix products, arithmetic and copies ran while one was open for 20% of the time, Pallas kernels for 0%

commit v1 on v0

v1 whole, which is shorter than its diff:
```python
import jax
import jax.numpy as jnp
from jax import lax
from jax.experimental import pallas as pl
from jax.experimental.pallas import tpu as pltpu
from jax.sharding import PartitionSpec as P

HEADS = 12
AXES = ("dp", "fsdp")
MASKED = -1000000000.0
EPSILON = 1e-06
F32 = jnp.float32
BF16 = jnp.bfloat16


def norm_forward(features, scaling, offset):
    center = features - jnp.mean(features, axis=-1, keepdims=True)
    inverse = lax.rsqrt(jnp.mean(center * center, axis=-1, keepdims=True) + EPSILON)
    normed = center * inverse
    return (normed * scaling.astype(F32) + offset.astype(F32), normed, inverse)


def norm_backward(upstream, normed, inverse, scaling):
    through = upstream * scaling.astype(F32)
    inward = inverse * (
        through
        - jnp.mean(through, axis=-1, keepdims=True)
        - normed * jnp.mean(through * normed, axis=-1, keepdims=True)
    )
    return (inward, jnp.sum(upstream * normed, axis=0), jnp.sum(upstream, axis=0))


def sums(equation, left, right):
    return jnp.einsum(equation, left, right, preferred_element_type=F32)


def layer(weights, patches, indices, counts, cotangent):
    qkv_full, out_full, up_full, down_full, first_gain, first_shift, second_gain, second_shift = weights
    strips, visible, patch_count = (indices.shape[0], indices.shape[1], patches.shape[1])
    width = out_full.shape[1]
    rows = strips * visible
    heads = (strips, visible, HEADS, width // HEADS)
    scale = (width // HEADS) ** (-0.5)
    present = jnp.arange(visible)[None, :] < counts[:, None]
    onehot = ((indices[:, :, None] == jnp.arange(patch_count)[None, None, :]) & present[:, :, None]).astype(BF16)
    inputs = sums("bvp,bpd->bvd", onehot, patches).reshape(rows, width)
    first_norm, first_normed, first_inverse = norm_forward(inputs, first_gain, first_shift)
    first_low = first_norm.astype(BF16)
    projected = jnp.dot(first_low, qkv_full, preferred_element_type=F32).astype(BF16)
    queries = projected[:, :width].reshape(heads)
    keys = projected[:, width : 2 * width].reshape(heads)
    values = projected[:, 2 * width :].reshape(heads)
    scores = sums("bqhe,bkhe->bhqk", queries, keys) * scale
    scores = jnp.where(present[:, None, None, :], scores, MASKED)
    attention = jax.nn.softmax(scores, axis=-1)
    attention_low = attention.astype(BF16)
    mixed = sums("bhqk,bkhe->bqhe", attention_low, values).astype(BF16).reshape(rows, width)
    middle = inputs + jnp.dot(mixed, out_full, preferred_element_type=F32)
    second_norm, second_normed, second_inverse = norm_forward(middle, second_gain, second_shift)
    second_low = second_norm.astype(BF16)
    hidden_pre = jnp.dot(second_low, up_full, preferred_element_type=F32)
    hidden, gelu_pull = jax.vjp(lambda v: jax.nn.gelu(v, approximate=False), hidden_pre)
    hidden_low = hidden.astype(BF16)
    branch = jnp.dot(hidden_low, down_full, preferred_element_type=F32)
    live = present.reshape(rows, 1)
    output = ((middle + branch) * live.astype(F32)).reshape(strips, visible, width)

    upstream = cotangent.reshape(rows, width) * live.astype(BF16)
    down_grad = sums("rf,rd->fd", hidden_low, upstream)
    pre_low = gelu_pull(sums("rd,fd->rf", upstream, down_full))[0].astype(BF16)
    up_grad = sums("rf,rd->fd", second_low, pre_low)
    second_back = sums("rd,fd->rf", pre_low, up_full)
    inward, second_gain_grad, second_shift_grad = norm_backward(second_back, second_normed, second_inverse, second_gain)
    middle_grad = upstream.astype(F32) + inward
    middle_low = middle_grad.astype(BF16)
    out_grad = sums("rf,rd->fd", mixed, middle_low)
    mixed_grad = sums("rd,fd->rf", middle_low, out_full).astype(BF16).reshape(heads)
    prob_grad = sums("bqhe,bkhe->bhqk", mixed_grad, values)
    value_grad = sums("bhqk,bqhe->bkhe", attention_low, mixed_grad)
    score_low = (attention * (prob_grad - jnp.sum(attention * prob_grad, axis=-1, keepdims=True))).astype(BF16)
    query_grad = sums("bhqk,bkhe->bqhe", score_low, keys) * scale
    key_grad = sums("bhqk,bqhe->bkhe", score_low, queries) * scale
    projected_grad = jnp.concatenate([g.reshape(rows, width) for g in (query_grad, key_grad, value_grad)], axis=1).astype(BF16)
    qkv_grad = sums("rf,rd->fd", first_low, projected_grad)
    first_back = sums("rd,fd->rf", projected_grad, qkv_full)
    inward, first_gain_grad, first_shift_grad = norm_backward(first_back, first_normed, first_inverse, first_gain)
    input_low = (middle_grad + inward).astype(BF16).reshape(strips, visible, width)
    patch_part = sums("bvp,bvd->bpd", onehot, input_low)
    gradients = (qkv_grad, out_grad, up_grad, down_grad, first_gain_grad, first_shift_grad, second_gain_grad, second_shift_grad)
    return (output, gradients, patch_part)


def any_slice(patches, visible_index, visible_count, *rest):
    weights, cotangent = rest[:-1], rest[-1]
    whole = [lax.all_gather(w, AXES, axis=0, tiled=True) for w in weights]
    micro, strips = patches.shape[:2]
    flat = lambda a: a.reshape((micro * strips,) + a.shape[2:])
    output, gradients, patch_part = layer(whole, flat(patches), flat(visible_index), flat(visible_count), flat(cotangent))
    shares = [lax.psum_scatter(g, AXES, scatter_dimension=0, tiled=True) for g in gradients]
    back = lambda a: a.reshape((micro, strips) + a.shape[1:])
    return (back(output), back(patch_part), *shares)


MESH = pl.DeviceIdType.MESH
EXT = 128
ROUNDS = 6


def coords():
    y = lax.axis_index("dp")
    f = lax.axis_index("fsdp")
    return y, f // 4, (f // 2) % 2, f % 2


def device(y, z, x, c):
    return (y, z * 4 + x * 2 + c)


def blocks(refs, rnd, par):
    first, second, third = refs
    if rnd == 0:
        return lambda *at: first.at[(par,) + at]
    if rnd < 4:
        return lambda *at: second.at[(2 * (rnd - 1) + par,) + at]
    return lambda yy, zz, xx, *at: third.at[(yy, zz, xx, 2 * par + (rnd - 4)) + at]


def cut(rnd):
    return 384, (512 if rnd == 0 else 384)


ALL = slice(None)


def other(z, dz):
    if dz == 0:
        return z
    if dz == 1:
        return z + 1 - 2 * (z % 2)
    if dz == 2:
        return (z + 2) % 4
    return 3 - z


class Gather:
    def __init__(self, place, weights, sems):
        self.place = place
        self.weights = weights
        self.sems = sems

    def copy(self, kind, i, src, dst, to):
        send, recv = self.sems[kind]
        return pltpu.make_async_remote_copy(src_ref=src, dst_ref=dst, send_sem=send.at[i], recv_sem=recv.at[i], device_id=to, device_id_type=MESH)

    def z(self, j, dz):
        y, z, x, c = self.place
        at = blocks(self.weights, j, c)
        return self.copy("z", (j, dz - 1), at(y, z, x), at(y, z, x), device(y, other(z, dz), x, c))

    def z_in(self, j, dz):
        y, z, x, c = self.place
        at = blocks(self.weights, j, c)
        there = at(y, other(z, dz), x)
        return self.copy("z", (j, dz - 1), there, there, device(y, other(z, dz), x, c))

    def side(self, j, dz, axis):
        y, z, x, c = self.place
        at = blocks(self.weights, j, c)
        src = at(y, other(z, dz), x)
        to = device(y, z, 1 - x, c) if axis == "x" else device(1 - y, z, x, c)
        return self.copy(axis, (j, dz), src, src, to)

    def side_in(self, j, dz, axis):
        y, z, x, c = self.place
        at = blocks(self.weights, j, c)
        there = at(y, other(z, dz), 1 - x) if axis == "x" else at(1 - y, other(z, dz), x)
        to = device(y, z, 1 - x, c) if axis == "x" else device(1 - y, z, x, c)
        return self.copy(axis, (j, dz), there, there, to)

    def diag(self, j, half):
        y, z, x, c = self.place
        at = blocks(self.weights, j, c)
        na, nb = cut(j)
        if half == 0:
            src = at(y, ALL, 1 - x, ALL, pl.ds(0, na))
            to = device(1 - y, z, x, c)
        else:
            src = at(1 - y, ALL, x, ALL, pl.ds(na, nb))
            to = device(y, z, 1 - x, c)
        return self.copy("g", (j, half), src, src, to)

    def diag_in(self, j, half):
        y, z, x, c = self.place
        at = blocks(self.weights, j, c)
        na, nb = cut(j)
        there = at(1 - y, ALL, 1 - x, ALL, pl.ds(0, na) if half == 0 else pl.ds(na, nb))
        to = device(1 - y, z, x, c) if half == 0 else device(y, z, 1 - x, c)
        return self.copy("g", (j, half), there, there, to)

    def down(self, j, q, par=None):
        y, z, x, c = self.place
        at = blocks(self.weights, j, c if par is None else par)
        yy = y if q < 2 else 1 - y
        xx = x if q % 2 == 0 else 1 - x
        src = at(yy, ALL, xx)
        return self.copy("d", (j, q), src, src, device(y, z, x, 1 - c))

    def down_in(self, j, q):
        return self.down(j, q, 1 - self.place[3])

    def begin(self, j):
        for dz in (1, 2, 3):
            self.z(j, dz).start()
        self.side(j, 0, "x").start()
        self.side(j, 0, "y").start()

    def forward(self, j):
        for dz in (1, 2, 3):
            self.z_in(j, dz).wait_recv()
            self.side(j, dz, "x").start()
            self.side(j, dz, "y").start()
        self.down(j, 0).start()

    def cross(self, j):
        for dz in range(4):
            self.side_in(j, dz, "x").wait_recv()
        self.diag(j, 0).start()
        self.down(j, 1).start()
        for dz in range(4):
            self.side_in(j, dz, "y").wait_recv()
        self.diag(j, 1).start()
        self.down(j, 2).start()

    def finish(self, j):
        self.diag_in(j, 0).wait_recv()
        self.diag_in(j, 1).wait_recv()
        self.down(j, 3).start()

    def arrive(self, j):
        for q in range(4):
            self.down_in(j, q).wait_recv()

    def sent(self, j):
        for dz in (1, 2, 3):
            self.z(j, dz).wait_send()
        for dz in range(4):
            self.side(j, dz, "x").wait_send()
            self.side(j, dz, "y").wait_send()
        self.diag(j, 0).wait_send()
        self.diag(j, 1).wait_send()
        for q in range(4):
            self.down(j, q).wait_send()


GATHER_SEMS = {"z": 3, "x": 4, "y": 4, "g": 2, "d": 4}


class Scatter:
    def __init__(self, place, sums, bufs, sems):
        self.place = place
        self.sums = sums
        self.bufs = bufs
        self.sems = sems

    def copy(self, kind, i, src, dst, to):
        send, recv = self.sems[kind]
        return pltpu.make_async_remote_copy(src_ref=src, dst_ref=dst, send_sem=send.at[i], recv_sem=recv.at[i], device_id=to, device_id_type=MESH)

    def a(self, j):
        y, z, x, c = self.place
        src = blocks(self.sums, j, 1 - c)(ALL, ALL, ALL)
        return self.copy("a", (j,), src, self.bufs["a"](j), device(y, z, x, 1 - c))

    def b(self, j, half):
        y, z, x, c = self.place
        at = blocks(self.sums, j, c)
        na, nb = cut(j)
        if half == 0:
            return self.copy("b", (j, 0), at(1 - y, ALL, ALL, ALL, pl.ds(0, na)), self.bufs["b0"](j), device(1 - y, z, x, c))
        return self.copy("b", (j, 1), at(ALL, ALL, 1 - x, ALL, pl.ds(na, nb)), self.bufs["b1"](j), device(y, z, 1 - x, c))

    def c(self, j, half):
        y, z, x, c = self.place
        at = blocks(self.sums, j, c)
        na, nb = cut(j)
        if half == 0:
            return self.copy("c", (j, 0), at(y, ALL, 1 - x, ALL, pl.ds(0, na)), self.bufs["c0"](j), device(y, z, 1 - x, c))
        return self.copy("c", (j, 1), at(1 - y, ALL, x, ALL, pl.ds(na, nb)), self.bufs["c1"](j), device(1 - y, z, x, c))

    def d(self, j, dz):
        y, z, x, c = self.place
        at = blocks(self.sums, j, c)
        return self.copy("d", (j, dz - 1), at(y, other(z, dz), x), self.bufs["d"](j, dz), device(y, other(z, dz), x, c))

    def e(self, j):
        y, z, x, c = self.place
        return self.copy("e", (j,), self.bufs["f"](j).at[1 - c], self.bufs["e"](j), device(y, z, x, 1 - c))

    def begin(self, j):
        self.a(j).start()

    def add_a(self, j):
        y, z, x, c = self.place
        self.a(j).wait_recv()
        at = blocks(self.sums, j, c)
        got = self.bufs["a"](j)

        @pl.loop(0, 16)
        def _(i):
            yy, zz, xx = i // 8, (i // 2) % 4, i % 2
            own = at(yy, zz, xx)
            own[...] = (own[...].astype(jnp.float32) + got[yy, zz, xx].astype(jnp.float32)).astype(own.dtype)

        self.b(j, 0).start()
        self.b(j, 1).start()

    def add_b(self, j):
        y, z, x, c = self.place
        na, nb = cut(j)
        at = blocks(self.sums, j, c)
        self.b(j, 0).wait_recv()
        got = self.bufs["b0"](j)

        @pl.loop(0, 8)
        def _(i):
            zz, xx = i // 2, i % 2
            own = at(y, zz, xx, ALL, pl.ds(0, na))
            own[...] = (own[...].astype(jnp.float32) + got[zz, xx].astype(jnp.float32)).astype(own.dtype)

        self.c(j, 0).start()
        self.b(j, 1).wait_recv()
        got1 = self.bufs["b1"](j)

        @pl.loop(0, 8)
        def _(i):
            yy, zz = i // 4, i % 4
            own = at(yy, zz, x, ALL, pl.ds(na, nb))
            own[...] = (own[...].astype(jnp.float32) + got1[yy, zz].astype(jnp.float32)).astype(own.dtype)

        self.c(j, 1).start()

    def add_c(self, j):
        y, z, x, c = self.place
        na, nb = cut(j)
        at = blocks(self.sums, j, c)
        self.c(j, 0).wait_recv()
        self.c(j, 1).wait_recv()
        got0, got1 = self.bufs["c0"](j), self.bufs["c1"](j)

        @pl.loop(0, 4)
        def _(zz):
            own = at(y, zz, x, ALL, pl.ds(0, na))
            own[...] = (own[...].astype(jnp.float32) + got0[zz].astype(jnp.float32)).astype(own.dtype)
            own1 = at(y, zz, x, ALL, pl.ds(na, nb))
            own1[...] = (own1[...].astype(jnp.float32) + got1[zz].astype(jnp.float32)).astype(own1.dtype)

        for dz in (1, 2, 3):
            self.d(j, dz).start()

    def add_d(self, j):
        y, z, x, c = self.place
        for dz in (1, 2, 3):
            self.d(j, dz).wait_recv()
        total = blocks(self.sums, j, c)(y, z, x)[...].astype(jnp.float32)
        for dz in (1, 2, 3):
            total = total + self.bufs["d"](j, dz)[...].astype(jnp.float32)
        out = self.bufs["f"](j)
        if j < 4:
            out[0] = total[:24]
            out[1] = total[24:]
            self.e(j).start()
        else:
            out[...] = total

    def sent(self, j):
        self.a(j).wait_send()
        for half in (0, 1):
            self.b(j, half).wait_send()
            self.c(j, half).wait_send()
        for dz in (1, 2, 3):
            self.d(j, dz).wait_send()
        if j < 4:
            self.e(j).wait_send()


SCATTER_SEMS = {"a": 0, "b": 2, "c": 2, "d": 3, "e": 0}


def sem_shapes(table):
    return [pltpu.SemaphoreType.DMA((ROUNDS, n) if n else (ROUNDS,)) for n in table.values() for _ in (0, 1)]


def sem_dict(table, refs):
    return {k: (refs[2 * i], refs[2 * i + 1]) for i, k in enumerate(table)}


def barrier(place):
    y, z, x, c = place
    bar = pltpu.get_barrier_semaphore()
    peers = [device(y, z, x, 1 - c), device(y, z, 1 - x, c), device(1 - y, z, x, c)] + [device(y, other(z, dz), x, c) for dz in (1, 2, 3)]
    for p in peers:
        pl.semaphore_signal(bar, inc=1, device_id=p, device_id_type=MESH)
    pl.semaphore_wait(bar, len(peers))

W_SHAPES = [(2, 2, 4, 2, 48, 768 + EXT), (6, 2, 4, 2, 48, 768), (2, 4, 2, 4, 48, 768)]

def stage_shards(place, ins, weights, s0, r0, s0sem):
    y, z, x, c = place
    qkv, out, up, down, ext = ins
    def piece(p):
        if p < 3:
            v = qkv[:, 768 * p : 768 * (p + 1)].astype(jnp.float32)
            return jnp.concatenate([v, ext[...].astype(jnp.float32)], axis=1) if p < 2 else v
        if p == 3:
            return out[...].astype(jnp.float32)
        return up[:, 768 * (p - 4) : 768 * (p - 3)].astype(jnp.float32)
    def shard_copy(j):
        n = 896 if j == 0 else 768
        return pltpu.make_async_remote_copy(src_ref=s0.at[j, :, pl.ds(0, n)], dst_ref=r0.at[j, :, pl.ds(0, n)], send_sem=s0sem.at[0, j], recv_sem=s0sem.at[1, j], device_id=device(y, z, x, 1 - c), device_id_type=MESH)
    def send(j):
        n = 896 if j == 0 else 768
        even, odd = piece(2 * j), piece(2 * j + 1)
        s0[j, :, pl.ds(0, n)] = jnp.where(c == 0, odd, even)
        shard_copy(j).start()
    def build(j):
        n = 896 if j == 0 else 768
        even, odd = piece(2 * j), piece(2 * j + 1)
        mine = jnp.where(c == 0, even, odd)
        shard_copy(j).wait_recv()
        got = r0[j, :, pl.ds(0, n)]
        blk = jnp.where(c == 0, jnp.concatenate([mine, got], axis=0), jnp.concatenate([got, mine], axis=0))
        blocks(weights, j, c)(y, z, x)[...] = blk.astype(jnp.bfloat16)
    def build_down():
        for k in (0, 1):
            weights[2][y, z, x, 2 * c + k] = down[48 * k : 48 * (k + 1), :]
    return shard_copy, send, build, build_down

def gather_kernel(qkv, out, up, down, ext, o0, o1, od, w0, w1, wd, s0, r0, s0sem, osem, *sems):
    place = coords()
    sd = sem_dict(GATHER_SEMS, sems)
    weights = (w0, w1, wd)
    barrier(place)
    shard_copy, send, build, build_down = stage_shards(place, (qkv, out, up, down, ext), weights, s0, r0, s0sem)
    g = Gather(place, weights, sd)
    for j in range(4): send(j)
    for j in range(4):
        build(j); g.begin(j)
    build_down()
    g.begin(4); g.begin(5)
    for step in range(ROUNDS + 2):
        if step < ROUNDS: g.forward(step)
        if 0 <= step - 1 < ROUNDS: g.cross(step - 1)
        if 0 <= step - 2 < ROUNDS: g.finish(step - 2)
    for j in range(ROUNDS): g.arrive(j)
    cps = [pltpu.make_async_copy(a, b, osem.at[i]) for i, (a, b) in enumerate(((w0, o0), (w1, o1), (wd, od)))]
    for cp in cps: cp.start()
    for j in range(ROUNDS): g.sent(j)
    for j in range(4): shard_copy(j).wait_send()
    for cp in cps: cp.wait()

def gather_call(qkv, out, up, down, ext):
    return pl.pallas_call(
        gather_kernel,
        out_shape=[jax.ShapeDtypeStruct(s, jnp.bfloat16) for s in W_SHAPES],
        in_specs=[pl.BlockSpec(memory_space=pltpu.VMEM)] * 5,
        out_specs=[pl.BlockSpec(memory_space=pl.ANY)] * 3,
        scratch_shapes=[pltpu.VMEM(s, jnp.bfloat16) for s in W_SHAPES] + [pltpu.VMEM((4, 24, 896), jnp.float32)] * 2
        + [pltpu.SemaphoreType.DMA((2, 4)), pltpu.SemaphoreType.DMA((3,))] + sem_shapes(GATHER_SEMS),
        compiler_params=pltpu.CompilerParams(collective_id=0, has_side_effects=True, vmem_limit_bytes=40 * 2**20),
        name="gather_weights",
    )(qkv, out, up, down, ext)

def scatter_kernel(i0, i1, id_, o0, o1, od, g0, g1, gd, ra0, ra, b0a, b0, b1a, b1, c0a, c0, c1a, c1, rda, rd, fs0, fs, fd, re0, re, isem, *sems):
    place = coords()
    sd = sem_dict(SCATTER_SEMS, sems)
    sums = (g0, g1, gd)
    cps = [pltpu.make_async_copy(a, b, isem.at[i]) for i, (a, b) in enumerate(((i0, g0), (i1, g1), (id_, gd)))]
    for cp in cps: cp.start()
    barrier(place)
    def pick(first, rest):
        return lambda j: first.at[0] if j == 0 else rest.at[j - 1]
    bufs = {"a": pick(ra0, ra), "b0": pick(b0a, b0), "b1": pick(b1a, b1), "c0": pick(c0a, c0), "c1": pick(c1a, c1),
            "d": lambda j, dz: rda.at[dz - 1] if j == 0 else rd.at[j - 1, dz - 1],
            "f": lambda j: fs0 if j == 0 else (fs.at[j - 1] if j < 4 else fd.at[j - 4]),
            "e": lambda j: re0 if j == 0 else re.at[j - 1]}
    s = Scatter(place, sums, bufs, sd)
    for cp in cps: cp.wait()
    order = [4, 5, 2, 3, 1, 0]
    for j in order: s.begin(j)
    fns = [s.add_a, s.add_b, s.add_c, s.add_d]
    for step in range(ROUNDS + 3):
        for lag in range(4):
            i = step - lag
            if 0 <= i < ROUNDS: fns[lag](order[i])
    c = place[3]
    for j in range(4):
        s.e(j).wait_recv()
        own = bufs["f"](j)[c]
        got = bufs["e"](j)[...]
        o = o0 if j == 0 else o1
        base = 0 if j == 0 else 2 * (j - 1)
        o[base] = jnp.where(c == 0, own, got)
        o[base + 1] = jnp.where(c == 0, got, own)
    for k in (0, 1):
        od[48 * k : 48 * (k + 1), :] = fd[k]
    for j in range(ROUNDS): s.sent(j)

def scatter_call(g0, g1, gd):
    bf = lambda *s: pltpu.VMEM(s, jnp.bfloat16)
    f = lambda *s: pltpu.VMEM(s, jnp.float32)
    return pl.pallas_call(
        scatter_kernel,
        out_shape=[jax.ShapeDtypeStruct((2, 24, 896), jnp.float32), jax.ShapeDtypeStruct((6, 24, 768), jnp.float32), jax.ShapeDtypeStruct((96, 768), jnp.float32)],
        in_specs=[pl.BlockSpec(memory_space=pl.ANY)] * 3,
        out_specs=[pl.BlockSpec(memory_space=pltpu.VMEM)] * 3,
        scratch_shapes=[bf(*s) for s in W_SHAPES] + [
            bf(1, 2, 4, 2, 48, 896), bf(5, 2, 4, 2, 48, 768),
            bf(1, 4, 2, 48, 384), bf(5, 4, 2, 48, 384),
            bf(1, 2, 4, 48, 512), bf(5, 2, 4, 48, 384),
            bf(1, 4, 48, 384), bf(5, 4, 48, 384),
            bf(1, 4, 48, 512), bf(5, 4, 48, 384),
            bf(3, 48, 896), bf(5, 3, 48, 768),
            f(2, 24, 896), f(3, 2, 24, 768), f(2, 48, 768),
            f(24, 896), f(3, 24, 768),
            pltpu.SemaphoreType.DMA((3,))] + sem_shapes(SCATTER_SEMS),
        compiler_params=pltpu.CompilerParams(collective_id=1, has_side_effects=True, vmem_limit_bytes=56 * 2**20),
        name="scatter_sums",
    )(g0, g1, gd)


def one_slice(patches, visible_index, visible_count, qkv_weight, out_weight, up_weight, down_weight, attention_gain, attention_shift, feedforward_gain, feedforward_shift, cotangent):
    small = jnp.stack([attention_gain, attention_shift, feedforward_gain, feedforward_shift], axis=1)
    ext = jnp.pad(small, ((0, 0), (0, EXT - 4)))
    w0, w1, wd = gather_call(qkv_weight, out_weight, up_weight, down_weight, ext)
    w0 = w0.reshape(2, 768, 768 + EXT)
    w1 = w1.reshape(6, 768, 768)
    gains = w0[0][:, 768:772]
    weights = (
        jnp.concatenate([w0[0][:, :768], w0[1][:, :768], w1[0]], axis=1),
        w1[1],
        jnp.concatenate([w1[2], w1[3], w1[4], w1[5]], axis=1),
        wd.reshape(3072, 768),
        gains[:, 0], gains[:, 1], gains[:, 2], gains[:, 3],
    )
    micro = patches.shape[0]
    strip = lambda a: a.reshape((micro,) + a.shape[2:])
    output, gradients, patch_part = layer(weights, strip(patches), strip(visible_index), strip(visible_count), strip(cotangent))
    qkv, out, up, down = [g.astype(jnp.bfloat16) for g in gradients[:4]]
    side = jnp.pad(jnp.stack(gradients[4:], axis=1), ((0, 0), (0, EXT - 4))).astype(jnp.bfloat16)
    g0 = jnp.stack([jnp.concatenate([qkv[:, 0:768], side], axis=1), jnp.concatenate([qkv[:, 768:1536], side], axis=1)]).reshape(W_SHAPES[0])
    g1 = jnp.stack([qkv[:, 1536:], out, up[:, :768], up[:, 768:1536], up[:, 1536:2304], up[:, 2304:]]).reshape(W_SHAPES[1])
    o0, o1, od = scatter_call(g0, g1, down.reshape(W_SHAPES[2]))
    return (
        output.reshape((micro, 1) + output.shape[1:]),
        patch_part.reshape((micro, 1) + patch_part.shape[1:]),
        jnp.concatenate([o0[0][:, :768], o0[1][:, :768], o1[0]], axis=1),
        o1[1],
        jnp.concatenate([o1[2], o1[3], o1[4], o1[5]], axis=1),
        od,
        o0[0][:, 768], o0[0][:, 769], o0[0][:, 770], o0[0][:, 771],
    )


def solution(mesh):
    strips = lambda n: P(None, AXES, *([None] * n))
    rows, row = P(AXES, None), P(AXES)
    body = one_slice if tuple(mesh.shape.values()) == (2, 16) else any_slice
    return jax.shard_map(
        body,
        mesh=mesh,
        in_specs=(strips(2), strips(1), strips(0), rows, rows, rows, rows, row, row, row, row, strips(2)),
        out_specs=(strips(2), strips(2), rows, rows, rows, rows, row, row, row, row),
        check_vma=False,
    )
```

time: 867 us -> 447 us (0.52)
  waiting for transfers between devices: 503 us -> 0 us
  Pallas kernels: 0 us -> 158 us
  blocking collectives: 82.4 us -> 0 us
  local copies, waits for them, and re-layouts: 40.2 us -> 96.1 us
  matrix products: 188 us -> 139 us
  between operations: 15.7 us -> 1.93 us
  other arithmetic: 32.7 us -> 42.3 us
    reduce_scatter x4 -> x0, waiting for transfers between devices: 381 us -> none  [the longest x1 142 us: per_device(): lax.psum_scatter(gradients[3], ('dp', 'fsdp'), scatter_dimension=0, tiled...]
    pallas_call x0 -> x2, Pallas kernels: none -> 158 us  [the longest x1 84.8 us: scatter_call(): pl.pallas_call(scatter_kernel, out_shape=[jax.ShapeDtypeStruct((2, 24, 89...]
    all_gather x4 -> x0, waiting for transfers between devices: 120 us -> none  [the longest x1 49.5 us: per_device(): lax.all_gather(down_weight, ('dp', 'fsdp'), axis=0, tiled=True)]
    unnamed x2 -> x0, blocking collectives: 82.4 us -> none
    dot_general x38 -> x19, matrix products: 170 us -> 127 us  [the longest x15 105 us: sums(): return jnp.einsum(equation, left, right, preferred_element_type=F32)]
    reshape x0 -> x12, local copies, waits for them, and re-layouts: none -> 42.1 us  [the longest x2 9.88 us: layer(): values = projected[:, 2 * width:].reshape(heads)]
    unnamed x155 -> x170, local copies, waits for them, and re-layouts: 14.1 us -> 26.5 us
    slice x11, local copies, waits for them, and re-layouts: 22.7 us -> 14 us  [the longest x1 6.19 us: one_slice(): w1[2]]
  transfers between devices with their start and end apart: 8 -> 0, of which waited for: 7 -> 0; matrix products, arithmetic and copies ran while one was open for 20% -> 0% of each run, Pallas kernels for 0% -> 0%
where the time goes in v1:
time: 447 us; the launch traced here: 438 us
  Pallas kernels  158 us (35%)
  matrix products  139 us (31%)
  local copies, waits for them, and re-layouts  96.1 us (21%)
  other arithmetic  42.3 us (9%)
    dot_general x15, matrix products, sums(): return jnp.einsum(equation, left, right, preferred_element_type=F32)  105 us
    pallas_call x1, Pallas kernels, scatter_call(): pl.pallas_call(scatter_kernel, out_shape=[jax.ShapeDtypeStruct((2, 24, 89...  84.8 us
    pallas_call x1, Pallas kernels, gather_call(): pl.pallas_call(gather_kernel, out_shape=[jax.ShapeDtypeStruct(s, jnp.bflo...  73.6 us
    unnamed x170, local copies, waits for them, and re-layouts  26.5 us
    convert_element_type x1, other arithmetic, layer(): (attention * (prob_grad - jnp.sum(attention * prob_grad, axis=-1, keepdim...  14 us
    sub x1, matrix products, layer(): attention = jax.nn.softmax(scores, axis=-1)  12.5 us
    convert_element_type x1, other arithmetic, layer(): hidden_low = hidden.astype(BF16)  11.4 us
    dot_general x1, matrix products, layer(): branch = jnp.dot(hidden_low, down_full, preferred_element_type=F32)  10.1 us

profile of v1, /device:TPU:0, one launch (start us, length us, event | category | flops | bytes accessed | tf_op | source)
XLA Modules:
  0.0 438.3 jit_solution(742279433635099147)
XLA Ops:
  13.3 73.6 %gather_weights.1 = (bf16[2,2,4,2,48,896]{5,4,3,2,1,0:T(8,128)(2,1)S(1)}, bf16[6,2,4,2,48,768]{5,4,3,2,1,0:T(8,128)(2,1)}, bf16[2,4,2,4,48,768]{5,4,3,2,1,0:T(8,128)(2,1)S(1)}) custom-call(bf16[24,2304]{1,0:T(8,128)(2,1)S(1)} %copy-done.4, bf16[24,768]{1,0:T(8,128)(2,1)S(1)} %copy-done.5, bf16[24,3072]{1,0:T(8,128)(2,1)S(1)} %copy-done.2, ...), custom_call_target="tpu_custom_call" | custom-call | tf_op jit(solution)/shard_map/gather_weights/pallas_call | solution.py:462
  93.4 6.2 %fusion.61 = (bf16[1,2,4,2,48,768]{5,4,3,2,1,0:T(8,128)(2,1)}, bf16[1,2,4,2,48,768]{5,4,3,2,1,0:T(8,128)(2,1)}, bf16[1,2,4,2,48,768]{5,4,3,2,1,0:T(8,128)(2,1)},...) fusion(bf16[6,2,4,2,48,768]{5,4,3,2,1,0:T(8,128)(2,1)} %get-tup, ...), kind=kLoop, calls=%fused_computation.133 | loop fusion | bytes 14155776 | tf_op jit(solution)/shard_map/slice | solution.py:541
  108.1 4.0 copy.84
  115.4 4.0 copy.83
  119.4 5.0 %reshape.292 = bf16[2,400,12,64]{3,2,1,0:T(8,128)(2,1)} reshape(bf16[800,768]{1,0:T(8,128)(2,1)} %get-tuple-element.80) | data formatting | bytes 2457600 | tf_op jit(solution)/shard_map/reshape | solution.py:52
  124.4 4.8 %copy.85 = bf16[2,400,12,64]{1,3,2,0:T(8,128)(2,1)} copy(bf16[2,400,12,64]{3,2,1,0:T(8,128)(2,1)} %reshape.292) | data formatting | bytes 2457600 | tf_op jit(solution)/shard_map/reshape | solution.py:52
  129.3 12.5 %fusion.68 = (f32[2,12,400]{2,1,0:T(8,128)S(1)}, f32[2,12,400,400]{2,3,1,0:T(8,128)}) fusion(pred[2,400]{1,0:T(4,128)(4,1)S(1)} %get-tuple-element.102, bf16[2,400,12,64]{1,3,2,0:T(8,128)(2,1)S(1)} %copy.83, bf16[2,400,12,64]{1,3,2,0:T(8,128)(2,1)S(1)} %copy.84), kind=kOutput, calls=%fused_computation.140 | convolution fusion | flops 506880384 | bytes 17856800 | tf_op jit(solution)/shard_map/sub | solution.py:55
  141.8 9.0 %fusion.36 = bf16[2,400,12,64]{1,3,2,0:T(8,128)(2,1)S(1)} fusion(bf16[2,400,12,64]{1,3,2,0:T(8,128)(2,1)} %copy.85, f32[2,12,400,400]{2,3,1,0:T(8,128)} %get-tuple-element.106, f32[2,12,400]{2,1,0:T(8,128)S(1)} %get-tuple-element.105), kind=kOutput, calls=%fused_computation.70 | convolution fusion | flops 499814400 | bytes 17856000 | tf_op jit(solution)/shard_map/bhqk,bkhe->bqhe/dot_general | solution.py:34
  160.2 4.1 fusion.49
  164.4 27.2 %add_convert_fusion = (bf16[800,3072]{1,0:T(8,128)(2,1)}, f32[800,3072]{1,0:T(8,128)}) fusion(f32[800,3072]{1,0:T(8,128)S(1)} %fusion.49, bf16[800,768]{1,0:T(8,128)(2,1)S(1)} %bitcast.122, bf16[3072,768]{1,0:T(8,128)(2,1)S(1)} %bitcast.106), kind=kOutput, calls=%fused_computation.8 | convolution fusion | flops 3951820800 | bytes 30523392 | tf_op jit(solution)/shard_map/rd,fd->rf/dot_general | solution.py:34
  191.7 8.9 %multiply_reduce_fusion.1 = (bf16[768]{0:T(1024)(128)(2,1)S(1)}, f32[800]{0:T(1024)S(1)}, f32[800]{0:T(1024)S(1)}, bf16[768]{0:T(1024)(128)(2,1)S(1)}, f32[800,768]{1,0:T(8,128)}) fusion(f32[800,768]{1,0:T(8,128)} %copy-done.12, f32[800]{0:T(1024)} %copy-done.62, f32[800]{0:T(1024)} %copy-done.52, f32[768]{0:T(1024)S(1)} %copy-done.61, ...), kind=kOutput, calls=%fused_computation.42 | convolution fusion | flops 3799274496 | bytes 14567936 | tf_op jit(solution)/shard_map/rd,fd->rf/dot_general | solution.py:34
  200.6 11.4 %multiply_convert_fusion.1 = bf16[800,3072]{1,0:T(8,128)(2,1)} fusion(f32[800,3072]{1,0:T(8,128)} %get-tuple-element.67, f32[800,3072]{1,0:T(8,128)} %copy-done.14), kind=kLoop, calls=%fused_computation.9 | loop fusion | flops 7372800 | bytes 24576000 | tf_op jit(solution)/shard_map/convert_element_type | solution.py:63
  212.0 10.1 %add_multiply_fusion = f32[800,768]{1,0:T(8,128)} fusion(f32[800,768]{1,0:T(8,128)} %copy-done.12, bf16[800,3072]{1,0:T(8,128)(2,1)} %multiply_convert_fusion.1, bf16[3072,768]{1,0:T(8,128)(2,1)} %bitcast.103, f32[800]{0:T(1024)S(1)} %copy-done.69), kind=kOutput, calls=%fused_computation.48 | convolution fusion | flops 3776102400 | bytes 14552192 | tf_op jit(solution)/shard_map/dot_general | solution.py:64
  222.1 6.4 %convolution_convert_fusion.2 = bf16[768,3072]{1,0:T(8,128)(2,1)S(1)} fusion(bf16[800,3072]{1,0:T(8,128)(2,1)S(1)} %bitcast.146, f32[800,768]{1,0:T(8,128)S(1)} %copy-done.13, f32[768]{0:T(1024)S(1)} %copy-done.66, f32[768]{0:T(1024)S(1)} %copy-done.61, f32[800]{0:T(1024)S(1)} %copy-done.63, f32[800]{0:T(1024)S(1)} %copy-done.53), kind=kOutput, calls=%fused_computation.29 | convolution fusion | flops 3780304896 | bytes 12103936 | tf_op jit(solution)/shard_map/rf,rd->fd/dot_general | solution.py:34
  237.0 6.9 %convolution_convert_fusion.1 = bf16[3072,768]{1,0:T(8,128)(2,1)} fusion(bf16[800,3072]{1,0:T(8,128)(2,1)S(1)} %bitcast.114, bf16[800,768]{1,0:T(8,128)(2,1)S(1)} %get-tuple-element.65), kind=kOutput, calls=%fused_computation.28 | convolution fusion | flops 3777232896 | bytes 10862592 | tf_op jit(solution)/shard_map/rf,rd->fd/dot_general | solution.py:34
  248.4 4.0 copy.91
  253.6 9.6 %fusion.33 = bf16[2,400,12,64]{1,3,2,0:T(8,128)(2,1)S(1)} fusion(bf16[2,400,12,64]{1,3,2,0:T(8,128)(2,1)S(1)} %copy.91, f32[2,12,400,400]{2,3,1,0:T(8,128)} %get-tuple-element.106, f32[2,12,400]{2,1,0:T(8,128)S(1)} %copy-done.51), kind=kOutput, calls=%fused_computation.69 | convolution fusion | flops 499814400 | bytes 17856000 | tf_op jit(solution)/shard_map/bhqk,bqhe->bkhe/dot_general | solution.py:34
  267.0 13.5 %multiply_reduce_fusion = (f32[2,12,400]{2,1,0:T(8,128)S(1)}, f32[2,12,400,400]{2,3,1,0:T(8,128)}) fusion(f32[2,12,400,400]{2,3,1,0:T(8,128)} %get-tuple-element.106, f32[2,12,400]{2,1,0:T(8,128)S(1)} %copy-done.51, bf16[2,400,12,64]{1,3,2,0:T(8,128)(2,1)} %copy-done.27, bf16[2,400,12,64]{1,3,2,0:T(8,128)(2,1)S(1)} %copy-done.26), kind=kOutput, calls=%fused_computation.2 | convolution fusion | flops 503030400 | bytes 33254400 | tf_op jit(solution)/shard_map/bqhe,bkhe->bhqk/dot_general | solution.py:34
  280.5 14.0 %multiply_convert_fusion = bf16[2,12,400,400]{2,3,1,0:T(8,128)(2,1)S(1)} fusion(f32[2,12,400,400]{2,3,1,0:T(8,128)} %get-tuple-element.111, f32[2,12,400]{2,1,0:T(8,128)S(1)} %get-tuple-element.110, f32[2,12,400,400]{2,3,1,0:T(8,128)} %get-tuple-element.106, f32[2,12,400]{2,1,0:T(8,128)S(1)} %copy-done.51), kind=kLoop, calls=%fused_computation.1 | loop fusion | flops 15360000 | bytes 38476800 | tf_op jit(solution)/shard_map/convert_element_type | solution.py:80
  302.2 4.8 %reshape.280 = bf16[800,768]{0,1:T(8,128)(2,1)} reshape(bf16[2,400,12,64]{1,0,3,2:T(2,128)(2,1)} %copy.95) | data formatting | bytes 2457600 | tf_op jit(solution)/shard_map/reshape | solution.py:83
  314.7 6.1 %multiply_reduce_fusion.2 = (bf16[768]{0:T(1024)(128)(2,1)S(1)}, f32[800]{0:T(1024)S(1)}, f32[800]{0:T(1024)S(1)}, bf16[768]{0:T(1024)(128)(2,1)S(1)}, f32[800,768]{1,0:T(8,128)S(1)}) fusion(f32[800]{0:T(1024)S(1)} %copy-done.59, f32[800]{0:T(1024)S(1)} %copy-done.57, f32[2,400,768]{2,1,0:T(8,128)S(1)} %copy-done.7, f32[800,768]{1,0:T(8,128)S(1)} %bitcast.108, ...), kind=kOutput, calls=%fused_computation.43 | convolution fusion | flops 2848527360 | bytes 14617088 | tf_op jit(solution)/shard_map/rd,fd->rf/dot_general | solution.py:34
  320.8 4.2 convolution_convert_fusion.3
  335.3 5.0 %copy.104 = f32[2,1,529,768]{3,1,2,0:T(1,128)} copy(f32[2,1,529,768]{3,2,0,1:T(8,128)S(1)} %fusion.23) | data formatting | bytes 6500352
  347.6 84.8 %scatter_sums.1 = (f32[2,24,896]{2,1,0:T(8,128)}, f32[6,24,768]{2,1,0:T(8,128)}, f32[96,768]{1,0:T(8,128)}) custom-call(bf16[2,2,4,2,48,896]{5,4,3,2,1,0:T(8,128)(2,1)} %pad_maximum_fusion.2.i0, bf16[6,2,4,2,48,768]{5,4,3,2,1,0:T(8,128)(2,1)} %constant_dynamic-update-slice_fusion.3.i1, bf16[2,4,2,4,48,768]{5,4,3,2,1,0:T(8,128)(2,1)} %bitcast.120), custom_call_target="tpu_custom_call" | custom-call | tf_op jit(solution)/shard_map/scatter_sums/pallas_call | solution.py:511
  (238 shorter events, 96.1 us)
Async XLA Ops:
  4.3 125.0 %copy-start.70 = (pred[2,400]{1,0:T(4,128)(4,1)}, pred[2,400]{1,0:T(4,128)(4,1)S(1)}, u32[]{:S(2)}) copy-start(pred[2,400]{1,0:T(4,128)(4,1)S(1)} %get-tuple-element.102) | copy-start | bytes 2404
  11.0 80.3 %copy-start.56 = (f32[800]{0:T(1024)}, f32[800]{0:T(1024)S(1)}, u32[]{:S(2)}) copy-start(f32[800]{0:T(1024)S(1)} %div.35) | copy-start | bytes 9604
  13.3 78.0 %copy-start.58 = (f32[800]{0:T(1024)}, f32[800]{0:T(1024)S(1)}, u32[]{:S(2)}) copy-start(f32[800]{0:T(1024)S(1)} %rsqrt.20) | copy-start | bytes 9604
  89.2 10.4 %copy-start.45 = (bf16[768,768]{1,0:T(8,128)(2,1)}, bf16[768,768]{1,0:T(8,128)(2,1)S(1)}, u32[]{:S(2)}) copy-start(bf16[768,768]{1,0:T(8,128)(2,1)S(1)} %slice.173) | copy-start | bytes 3538948
  91.2 66.9 %copy-start.60 = (f32[768]{0:T(1024)}, f32[768]{0:T(1024)S(1)}, u32[]{:S(2)}) copy-start(f32[768]{0:T(1024)S(1)} %get-tuple-element.116) | copy-start | bytes 9220
  91.2 66.9 %copy-start.65 = (f32[768]{0:T(1024)}, f32[768]{0:T(1024)S(1)}, u32[]{:S(2)}) copy-start(f32[768]{0:T(1024)S(1)} %get-tuple-element.115) | copy-start | bytes 9220
  112.1 17.2 %copy-start.8 = (bf16[2,400,12,64]{1,3,2,0:T(8,128)(2,1)}, bf16[2,400,12,64]{1,3,2,0:T(8,128)(2,1)S(1)}, u32[]{:S(2)}) copy-start(bf16[2,400,12,64]{1,3,2,0:T(8,128)(2,1)S(1)} %copy.84) | copy-start | bytes 3686404
  153.7 10.7 %slice-start = ((s8[4718592]{0:T(1024)(128)(4,1)}), s8[4194304]{0:T(1024)(128)(4,1)S(1)}, s32[]{:S(2)}) async-start(s8[4718592]{0:T(1024)(128)(4,1)} %bitcast.104), calls=%async_computation | async-start | bytes 8388608
  164.4 27.2 %copy-start.14 = (f32[800,3072]{1,0:T(8,128)}, f32[800,3072]{1,0:T(8,128)S(1)}, u32[]{:S(2)}) copy-start(f32[800,3072]{1,0:T(8,128)S(1)} %fusion.49) | copy-start | bytes 29491204
  164.4 27.2 %copy-start.38 = (bf16[1,2,4,2,48,768]{5,4,3,2,1,0:T(8,128)(2,1)S(1)}, bf16[1,2,4,2,48,768]{5,4,3,2,1,0:T(8,128)(2,1)}, u32[]{:S(2)}) copy-start(bf16[1,2,4,2,48,768]{5,4,3,2,1,0:T(8,128)(2,1)} %get-tuple-element.68) | copy-start | bytes 3538948
  164.4 27.2 %copy-start.40 = (bf16[1,2,4,2,48,768]{5,4,3,2,1,0:T(8,128)(2,1)S(1)}, bf16[1,2,4,2,48,768]{5,4,3,2,1,0:T(8,128)(2,1)}, u32[]{:S(2)}) copy-start(bf16[1,2,4,2,48,768]{5,4,3,2,1,0:T(8,128)(2,1)} %get-tuple-element.69) | copy-start | bytes 3538948
  164.4 27.2 %copy-start.42 = (bf16[1,2,4,2,48,768]{5,4,3,2,1,0:T(8,128)(2,1)S(1)}, bf16[1,2,4,2,48,768]{5,4,3,2,1,0:T(8,128)(2,1)}, u32[]{:S(2)}) copy-start(bf16[1,2,4,2,48,768]{5,4,3,2,1,0:T(8,128)(2,1)} %get-tuple-element.70) | copy-start | bytes 3538948
  164.4 27.2 %copy-start.44 = (bf16[1,2,4,2,48,768]{5,4,3,2,1,0:T(8,128)(2,1)S(1)}, bf16[1,2,4,2,48,768]{5,4,3,2,1,0:T(8,128)(2,1)}, u32[]{:S(2)}) copy-start(bf16[1,2,4,2,48,768]{5,4,3,2,1,0:T(8,128)(2,1)} %get-tuple-element.71) | copy-start | bytes 3538948
  164.4 27.2 %copy-start.61 = (f32[768]{0:T(1024)S(1)}, f32[768]{0:T(1024)}, u32[]{:S(2)}) copy-start(f32[768]{0:T(1024)} %copy-done.60) | copy-start | bytes 9220
  200.6 11.4 %copy-start.69 = (f32[800]{0:T(1024)S(1)}, f32[800]{0:T(1024)}, u32[]{:S(2)}) copy-start(f32[800]{0:T(1024)} %reshape.290) | copy-start | bytes 9604
  200.6 21.5 %slice-start.4 = ((s8[4915200]{0:T(1024)(128)(4,1)}), s8[720896]{0:T(1024)(128)(4,1)S(1)}, s32[]{:S(2)}) async-start(s8[4915200]{0:T(1024)(128)(4,1)} %bitcast.145), calls=%async_computation.4 | async-start | bytes 1441792
  212.0 10.1 %copy-start.13 = (f32[800,768]{1,0:T(8,128)S(1)}, f32[800,768]{1,0:T(8,128)}, u32[]{:S(2)}) copy-start(f32[800,768]{1,0:T(8,128)} %copy-done.12) | copy-start | bytes 7372804
  212.0 10.1 %copy-start.53 = (f32[800]{0:T(1024)S(1)}, f32[800]{0:T(1024)}, u32[]{:S(2)}) copy-start(f32[800]{0:T(1024)} %copy-done.52) | copy-start | bytes 9604
  212.0 10.1 %copy-start.63 = (f32[800]{0:T(1024)S(1)}, f32[800]{0:T(1024)}, u32[]{:S(2)}) copy-start(f32[800]{0:T(1024)} %copy-done.62) | copy-start | bytes 9604
  212.0 10.1 %copy-start.66 = (f32[768]{0:T(1024)S(1)}, f32[768]{0:T(1024)}, u32[]{:S(2)}) copy-start(f32[768]{0:T(1024)} %copy-done.65) | copy-start | bytes 9220
  212.0 10.1 %slice-start.5 = ((s8[4915200]{0:T(1024)(128)(4,1)}), s8[4194304]{0:T(1024)(128)(4,1)S(1)}, s32[]{:S(2)}) async-start(s8[4915200]{0:T(1024)(128)(4,1)} %bitcast.145), calls=%async_computation.5 | async-start | bytes 8388608
  233.5 10.4 %copy-start.10 = (f32[800,768]{1,0:T(8,128)}, f32[800,768]{1,0:T(8,128)S(1)}, u32[]{:S(2)}) copy-start(f32[800,768]{1,0:T(8,128)S(1)} %get-tuple-element.64) | copy-start | bytes 7372804
  280.5 14.0 %copy-start.16 = (bf16[2,400,12,64]{1,3,2,0:T(8,128)(2,1)S(1)}, bf16[2,400,12,64]{1,3,2,0:T(8,128)(2,1)}, u32[]{:S(2)}) copy-start(bf16[2,400,12,64]{1,3,2,0:T(8,128)(2,1)} %copy-done.15) | copy-start | bytes 3686404
  347.6 90.5 %copy-start.1 = (bf16[2,1,529,768]{3,0,2,1:T(2,128)(2,1)S(1)}, bf16[2,1,529,768]{3,0,2,1:T(2,128)(2,1)}, u32[]{:S(2)}) copy-start(bf16[2,1,529,768]{3,0,2,1:T(2,128)(2,1)} %param.12) | copy-start | bytes 4875268
  (54 other events, 196.0 us)
